TPU v7x, 32 devices: a whole 2x2x4 slice. The times are simulated.
32 devices in a mesh: dp: 4 (over z), task: 4 (over y, core), mp: 2 (over x).
Axes of the slice: x: 2, y: 2, z: 4, core: 2. Of those that a mesh axis runs over, the one named last changes fastest.
Arguments:
- tokens: bfloat16 [3072, 2048], P(('dp', 'task')), may hold values from -6 to 6
- expert_ids: int32 [3072, 2], P(('dp', 'task')), may hold values from 0 to 3, all different within a row; in each aligned block of 192 rows (0 to 191, 192 to 383, ...) at most 120 rows name the same one
- gate_levels: int32 [3072, 2], P(('dp', 'task')), may hold values from 1 to 15
- expert_weight: bfloat16 [4, 2048, 4096], P('dp', None, 'mp'), may hold values from -0.125 to 0.125
- tower_weight: bfloat16 [4, 4096, 256], P(None, 'mp'), may hold values from -0.09375 to 0.09375
- tower_out: float32 [4, 256], P('task'), may hold values from -1.5 to 1.5
- cotangent: float32 [4, 3072], P('task', 'dp'), may hold values from -24 to 24
Outputs:
- predictions: float32 [4, 3072], P('task', 'dp')
- mix_grad: bfloat16 [3072, 4096], P(('dp', 'task'), 'mp')
Inputs may be any that keep to these rules, and one draw needn't show every extreme that they name: `expert_ids`: each row names 2 different experts; in each aligned block of 192 rows (the rows of one device) no expert is named by more than 120 rows, and some expert reaches 120 in some block.
All inputs are finite; a program needn't handle non-finite values.
Results may differ from a plain program's by a relative error of at most 0.02.
Values may be sent and summed in bfloat16 or wider, within the bound.
A program may use at most 64 MiB of HBM per device.

v0:
```python
import jax
import jax.numpy as jnp
from jax import lax
from jax.sharding import PartitionSpec as P


def body(tokens, expert_ids, gate_levels, expert_weight, tower_weight, tower_out, cotangent):
    experts_here = lax.axis_size("dp")
    tok_dev, top = expert_ids.shape
    width = tokens.shape[1]
    routes = tok_dev * top
    capacity = max(2, 5 * routes // (4 * experts_here))
    flat_ids = expert_ids.reshape(routes)
    onehot = (flat_ids[:, None] == jnp.arange(experts_here, dtype=jnp.int32)[None, :]).astype(
        jnp.int32
    )
    rank = jnp.cumsum(onehot, axis=0) - 1
    position = jnp.sum(onehot * rank, axis=1)
    dest = flat_ids * capacity + position
    token_rows = tokens[jnp.arange(routes, dtype=jnp.int32) // top]
    outgoing = jnp.zeros((experts_here * capacity, width), jnp.bfloat16).at[dest].set(token_rows)
    outgoing = outgoing.reshape(experts_here, capacity, width)
    own_weight = expert_weight[0]
    pre = jnp.einsum(
        "sid,dh->sih",
        lax.all_to_all(outgoing, "dp", split_axis=0, concat_axis=0, tiled=True),
        own_weight,
        preferred_element_type=jnp.float32,
    )
    hidden = jax.nn.silu(pre).astype(jnp.bfloat16)
    back = lax.all_to_all(hidden, "dp", split_axis=0, concat_axis=0, tiled=True)
    out_cols = back.shape[2]
    picked = back.reshape(experts_here * capacity, out_cols)[dest].reshape(tok_dev, top, out_cols)
    levels = gate_levels.astype(jnp.float32)
    gates = levels / jnp.sum(levels, axis=1, keepdims=True)
    mix = jnp.sum(picked.astype(jnp.float32) * gates[:, :, None], axis=1).astype(jnp.bfloat16)
    tower_index = lax.axis_index("task")
    own_tower = lax.dynamic_index_in_dim(tower_weight, tower_index, 0, keepdims=False)
    partial_z = jnp.dot(
        lax.all_gather(mix, "task", axis=0, tiled=True),
        own_tower,
        preferred_element_type=jnp.float32,
    )
    z_full = lax.psum(partial_z.astype(jnp.bfloat16), "mp").astype(jnp.float32)
    sig = jax.nn.sigmoid(z_full)
    out_vec = tower_out[0]
    predictions = jnp.dot(z_full * sig, out_vec, preferred_element_type=jnp.float32)[None, :]
    dz_rows = (
        cotangent[0][:, None] * out_vec[None, :] * sig * (1.0 + z_full * (1.0 - sig))
    ).astype(jnp.bfloat16)
    grad_sum = lax.psum_scatter(
        jnp.dot(dz_rows, own_tower.T, preferred_element_type=jnp.float32).astype(jnp.bfloat16),
        "task",
        scatter_dimension=0,
        tiled=True,
    )
    return (predictions, grad_sum)


def solution(mesh):
    return jax.shard_map(
        body,
        mesh=mesh,
        in_specs=(
            P(("dp", "task"), None),
            P(("dp", "task"), None),
            P(("dp", "task"), None),
            P("dp", None, "mp"),
            P(None, "mp", None),
            P("task", None),
            P("task", "dp"),
        ),
        out_specs=(P("task", "dp"), P(("dp", "task"), "mp")),
        check_vma=False,
    )
```

profile of v0, /device:TPU:0, one launch (start us, length us, event | category | flops | bytes accessed | tf_op | source)
XLA Modules:
  0.0 250.3 jit_solution(443442222776567292)
XLA Ops:
  7.2 0.0 copy-start
  7.2 0.9 copy.11
  8.1 0.1 eq.29
  8.2 0.1 eq.25
  8.3 0.7 broadcast_multiply_fusion
  9.1 1.2 reduce-window.6
  10.3 0.2 slice_reduce_fusion
  10.5 0.2 reduce-window.9
  10.7 0.1 add_bitcast_fusion
  10.8 0.1 copy.10
  10.9 0.1 mul.60
  11.1 0.0 copy-done
  11.1 8.4 %scatter_custom_fusion = bf16[480,2048]{1,0:T(8,128)(2,1)S(1)} fusion(s32[384]{0:T(512)S(1)} %fusion.27, bf16[192,2048]{1,0:T(8,128)(2,1)S(1)} %copy-done, s32[1024]{0:T(1024)S(1)} %pad_clamp_fusion.1, bf16[]{:T(256)} %constant.37.clone.1), kind=kCustom, calls=%fused_computation.8 | custom fusion | bytes 1966082 | tf_op jit(solution)/shard_map/scatter | solution.py:21
  19.5 51.5 %all_to_all.10 = bf16[4,120,2048]{2,1,0:T(8,128)(2,1)S(1)} all-to-all(bf16[4,120,2048]{2,1,0:T(8,128)(2,1)S(1)} %bitcast.44), channel_id=1, replica_groups=mesh['dp'=4,'task'=4,'mp'=2] {'dp'}, dimensions={0} | all-to-all | bytes 3932160 | tf_op jit(solution)/shard_map/all_to_all | solution.py:26
  71.0 9.0 %multiply_convert_fusion = bf16[4,120,2048]{2,1,0:T(8,128)(2,1)} fusion(bf16[4,120,2048]{2,1,0:T(8,128)(2,1)S(1)} %all_to_all.10, bf16[1,2048,2048]{2,1,0:T(8,128)(2,1)} %param.10), kind=kOutput, calls=%fused_computation.5 | convolution fusion | flops 4031447040 | bytes 12320768 | tf_op jit(solution)/shard_map/sid,dh->sih/dot_general | solution.py:24
  80.0 0.0 copy-start.1
  80.0 3.7 %all-to-all-start.1 = ((bf16[4,120,2048]{2,1,0:T(8,128)(2,1)}), bf16[4,120,2048]{2,1,0:T(8,128)(2,1)S(1)}, u32[]{:S(2)}, u32[]{:S(2)}) async-start(bf16[4,120,2048]{2,1,0:T(8,128)(2,1)} %multiply_convert_fusion), calls=%async_computation.1 | async-start | bytes 3932160 | tf_op jit(solution)/shard_map/all_to_all | solution.py:31
  83.8 0.2 all-gather.2.cloned.1.call-start
  84.0 0.0 copy-done.1
  84.0 0.1 copy.13
  84.2 44.1 %all-to-all-done.1 = bf16[4,120,2048]{2,1,0:T(8,128)(2,1)S(1)} async-done(((bf16[4,120,2048]{2,1,0:T(8,128)(2,1)}), bf16[4,120,2048]{2,1,0:T(8,128)(2,1)S(1)}, u32[]{:S(2)}, u32[]{:S(2)}) %all-to-all-start.1) | async-done | bytes 1966112 | tf_op jit(solution)/shard_map/all_to_all | solution.py:31
  128.3 3.1 %gather_fusion = bf16[384,2048]{1,0:T(8,128)(2,1)} fusion(bf16[480,2048]{1,0:T(8,128)(2,1)S(1)} %bitcast.43, s32[1024]{0:T(1024)S(1)} %pad_clamp_fusion), kind=kCustom, calls=%fused_computation.1 | custom fusion | bytes 3147264 | tf_op jit(solution)/shard_map/gather | solution.py:33
  131.4 4.7 %reshape.110 = f32[192,2,2048]{2,1,0:T(2,128)} reshape(bf16[384,2048]{1,0:T(8,128)(2,1)} %gather_fusion) | data formatting | bytes 4718592 | tf_op jit(solution)/shard_map/convert_element_type | solution.py:36
  136.1 7.8 %multiply_reduce_fusion = bf16[192,2048]{1,0:T(8,128)(2,1)} fusion(f32[192,2,2048]{2,1,0:T(2,128)} %reshape.110, f32[192,2]{1,0:T(8,128)S(1)} %copy.13), kind=kLoop, calls=%fused_computation.7 | loop fusion | flops 1179648 | bytes 3933696 | tf_op jit(solution)/shard_map/reduce_sum | solution.py:36
  143.9 0.0 all-gather.2.cloned.1.call-update
  143.9 0.0 copy-start.2
  143.9 0.0 copy-start.4
  143.9 0.0 all-reduce.2.cloned.1.call-start
  144.0 27.7 %all-gather.2.cloned.1.call-done = bf16[768,2048]{1,0:T(8,128)(2,1)} async-done(((bf16[192,2048]{1,0:T(8,128)(2,1)}), bf16[768,2048]{1,0:T(8,128)(2,1)}) %all-gather.2.cloned.1.call-update) | async-done | bytes 3145744 | tf_op jit(solution)/shard_map/all_gather | solution.py:40
  171.7 3.9 %convolution_convert_fusion.1 = bf16[768,256]{1,0:T(8,128)(2,1)} fusion(bf16[768,2048]{1,0:T(8,128)(2,1)} %all-gather.2.cloned.1.call-done, bf16[4,2048,256]{2,1,0:T(8,128)(2,1)} %param.11, s32[]{:T(128)S(6)} %select_n.40), kind=kOutput, calls=%fused_computation.10 | convolution fusion | flops 805502976 | bytes 4587524 | tf_op jit(solution)/shard_map/dot_general | solution.py:39
  175.6 0.0 all-reduce.2.cloned.1.call-update
  175.6 0.0 reduce-scatter.2.cloned.1.call-start
  175.6 0.0 copy-done.2
  175.7 25.8 %all-reduce.2.cloned.1.call-done = bf16[768,256]{1,0:T(8,128)(2,1)} async-done(((bf16[768,256]{1,0:T(8,128)(2,1)}), bf16[768,256]{1,0:T(8,128)(2,1)}) %all-reduce.2.cloned.1.call-update) | async-done | bytes 393232 | tf_op jit(solution)/shard_map/psum | solution.py:44
  201.5 0.0 copy-done.4
  201.5 4.2 %convolution_convert_fusion = bf16[768,2048]{1,0:T(8,128)(2,1)} fusion(bf16[4,2048,256]{2,1,0:T(8,128)(2,1)} %param.11, s32[]{:T(128)S(6)} %select_n.40, bf16[768,256]{1,0:T(8,128)(2,1)} %all-reduce.2.cloned.1.call-done, f32[256]{0:T(256)S(1)} %bitcast.46, f32[768]{0:T(1024)S(1)} %reduce.3), kind=kOutput, calls=%fused_computation.6 | convolution fusion | flops 809041920 | bytes 4591620 | tf_op jit(solution)/shard_map/dot_general | solution.py:52
  205.6 0.0 copy-start.3
  205.6 0.0 reduce-scatter.2.cloned.1.call-update
  205.7 1.0 copy-done.3
  206.6 0.9 fusion.14
  207.5 36.2 %reduce-scatter.2.cloned.1.call-done = bf16[192,2048]{1,0:T(8,128)(2,1)} async-done(((bf16[768,2048]{1,0:T(8,128)(2,1)}), bf16[192,2048]{1,0:T(8,128)(2,1)}) %reduce-scatter.2.cloned.1.call-update) | async-done | bytes 786448 | tf_op jit(solution)/shard_map/reduce_scatter | solution.py:51
  (9 shorter events, 0.1 us)
Async XLA Ops:
  7.2 3.9 %copy-start = (bf16[192,2048]{1,0:T(8,128)(2,1)S(1)}, bf16[192,2048]{1,0:T(8,128)(2,1)}, u32[]{:S(2)}) copy-start(bf16[192,2048]{1,0:T(8,128)(2,1)} %param.7) | copy-start | bytes 2359300
  80.0 4.0 %copy-start.1 = (s32[192,2]{0,1:T(2,128)S(1)}, s32[192,2]{0,1:T(2,128)}, u32[]{:S(2)}) copy-start(s32[192,2]{0,1:T(2,128)} %param.9) | copy-start | bytes 4612
  80.0 48.2 %all-to-all-start.1 = ((bf16[4,120,2048]{2,1,0:T(8,128)(2,1)}), bf16[4,120,2048]{2,1,0:T(8,128)(2,1)S(1)}, u32[]{:S(2)}, u32[]{:S(2)}) async-start(bf16[4,120,2048]{2,1,0:T(8,128)(2,1)} %multiply_convert_fusion), calls=%async_computation.1 | async-start | bytes 3932160 | tf_op jit(solution)/shard_map/all_to_all | solution.py:31
  83.8 87.9 %all-gather.2.cloned.1.call-start = ((), (), s32[]{:S(2)}) async-start(), calls=%async_computation.3 | async-start | bytes 3932160 | tf_op jit(solution)/shard_map/all_gather | solution.py:40
  143.9 31.8 %copy-start.2 = (f32[1,768]{1,0:T(1,128)S(1)}, f32[1,768]{1,0:T(1,128)}, u32[]{:S(2)}) copy-start(f32[1,768]{1,0:T(1,128)} %param.13) | copy-start | bytes 9220
  143.9 57.6 %copy-start.4 = (f32[1,256]{1,0:T(1,128)S(1)}, f32[1,256]{1,0:T(1,128)}, u32[]{:S(2)}) copy-start(f32[1,256]{1,0:T(1,128)} %param.12) | copy-start | bytes 3076
  143.9 57.6 %all-reduce.2.cloned.1.call-start = ((), (), s32[]{:S(2)}) async-start(), calls=%async_computation.4 | async-start | bytes 786432 | tf_op jit(solution)/shard_map/psum | solution.py:44
  175.6 68.2 %reduce-scatter.2.cloned.1.call-start = ((), (), s32[]{:S(2)}) async-start(), calls=%async_computation.5 | async-start | bytes 3932160 | tf_op jit(solution)/shard_map/reduce_scatter | solution.py:51
  205.6 1.0 copy-start.3
Sparse Core Ops, SparseCore 0:
  144.0 27.6 all-gather.1
  175.7 25.7 all-reduce.1
  205.8 37.9 reduce-scatter.1
where the time goes:
time: 251 us; the launch traced here: 250 us
  waiting for transfers between devices  134 us (53%)
  blocking collectives  51.5 us (21%)
  local copies, waits for them, and re-layouts  19 us (8%)
  matrix products  17.9 us (7%)
  between operations  13.9 us (6%)
  other arithmetic  10.1 us (4%)
  starting transfers between devices  4.03 us (2%)
    all_to_all x1, blocking collectives, body(): lax.all_to_all(outgoing, 'dp', split_axis=0, concat_axis=0, tiled=True)  51.5 us
    all_to_all x1, waiting for transfers between devices, body(): back = lax.all_to_all(hidden, 'dp', split_axis=0, concat_axis=0, tiled=True)  44.1 us
    reduce_scatter x1, waiting for transfers between devices, body(): lax.psum_scatter(jnp.dot(dz_rows, own_tower.T, preferred_element_type=jnp...  36.2 us
    all_gather x1, waiting for transfers between devices, body(): lax.all_gather(mix, 'task', axis=0, tiled=True)  27.7 us
    psum x1, waiting for transfers between devices, body(): z_full = lax.psum(partial_z.astype(jnp.bfloat16), 'mp').astype(jnp.float32)  25.8 us
    dot_general x1, matrix products, body(): jnp.einsum('sid,dh->sih', lax.all_to_all(outgoing, 'dp', split_axis=0, co...  8.97 us
    scatter x1, local copies, waits for them, and re-layouts, body(): jnp.zeros((experts_here * capacity, width), jnp.bfloat16).at[dest]  8.42 us
    reduce_sum x1, other arithmetic, body(): jnp.sum(picked.astype(jnp.float32) * gates[:, :, None], axis=1)  7.76 us
  transfers between devices with their start and end apart: 4, of which 4 were waited for; matrix products, arithmetic and copies ran while one was open for 0% of the time, Pallas kernels for 0%

commit v1 on v0

v1 whole, which is shorter than its diff:
```python
import functools

import jax
import jax.numpy as jnp
from jax import lax
from jax.experimental import pallas as pl
from jax.experimental.pallas import tpu as pltpu
from jax.sharding import PartitionSpec as P

MESH = pl.DeviceIdType.MESH
F32 = jnp.float32
BF16 = jnp.bfloat16


def sigmoid(v):
    return 0.5 + 0.5 * jnp.tanh(0.5 * v)


def kernel(
    n, nt, m,
    tokens, ids, levels, weight, towers, tower_out, cotangent,
    pred_out, grad_out,
    tok, w, tw, disp, held, gate, hid, part, rs_out, rs_in, back_out, back_in,
    zsum, dz, small_out, small_in, pred_send, pred_in,
    load_sem, z_send, z_recv, x_send, x_recv, rs_send, rs_recv, b_send, b_recv,
    s_send, s_recv, d_send, d_recv, p_send, p_recv,
):
    zi, ti, xi = lax.axis_index("dp"), lax.axis_index("task"), lax.axis_index("mp")
    rows = ids.shape[0]
    slots = gate.shape[2]
    depth = tok.shape[2]
    units = w.shape[1]
    ft = towers.shape[2]
    tl = nt // m
    ucols = tl * ft

    def partner(o):
        other, bit = 0, 1
        while bit < n:
            other = other + bit * ((zi // bit + o // bit) % 2)
            bit *= 2
        return other

    tok_loads = []
    for j in range(m):
        tok_loads.append(pltpu.make_async_copy(
            tokens.at[:, pl.ds(j * depth, depth)], tok.at[j], load_sem.at[2 + j]))
        tok_loads[j].start()
    w_load = pltpu.make_async_copy(weight.at[0], w, load_sem.at[0])
    tw_load = pltpu.make_async_copy(towers, tw, load_sem.at[1])
    w_load.start()
    tw_load.start()

    barrier = pltpu.get_barrier_semaphore()

    def greet_line(o, c):
        pl.semaphore_signal(barrier, inc=1, device_id={"dp": partner(o)}, device_id_type=MESH)
        return c

    def greet_plane(o, c):
        at = (ti * m + xi + o) % (nt * m)
        pl.semaphore_signal(
            barrier, inc=1, device_id={"task": at // m, "mp": at % m}, device_id_type=MESH)
        return c

    lax.fori_loop(1, n, greet_line, 0)
    lax.fori_loop(1, nt * m, greet_plane, 0)

    lane = lax.broadcasted_iota(jnp.int32, (rows, 128), 1)
    first, second = ids[:, 0:1] == lane, ids[:, 1:2] == lane
    level_of = (jnp.where(first, levels[:, 0:1], 0) + jnp.where(second, levels[:, 1:2], 0)).astype(F32)
    named = jnp.where(level_of > 0, 1.0, 0.0)
    above = jnp.where(
        lax.broadcasted_iota(jnp.int32, (rows, rows), 0)
        > lax.broadcasted_iota(jnp.int32, (rows, rows), 1), 1.0, 0.0)
    rank = jnp.dot(above.astype(BF16), named.astype(BF16), preferred_element_type=F32)
    place = jnp.where(named > 0, rank, -1.0)
    scale = 1.0 / jnp.sum(level_of, axis=1, keepdims=True)
    slot = lax.broadcasted_iota(jnp.int32, (rows, slots), 1).astype(F32)

    def pick(d):
        chosen = lane == d
        here = jnp.sum(jnp.where(chosen, place, 0.0), axis=1, keepdims=True)
        level = jnp.sum(jnp.where(chosen, level_of, 0.0), axis=1, keepdims=True)
        hit = slot == here
        gate[d] = jnp.where(hit, level, 0.0).astype(BF16)
        return jnp.where(hit, 1.0, 0.0).astype(BF16)

    def gathered(spot, j):
        return lax.dot_general(
            spot, tok[j], (((0,), (0,)), ((), ())), preferred_element_type=F32).astype(BF16)

    for j in range(m):
        tok_loads[j].wait()
    pl.semaphore_wait(barrier, n - 1 + nt * m - 1)

    def dispatch_copy(o):
        d = partner(o)
        return pltpu.make_async_remote_copy(
            src_ref=disp.at[d], dst_ref=held.at[zi, xi], send_sem=z_send.at[d],
            recv_sem=z_recv.at[zi], device_id={"dp": d}, device_id_type=MESH)

    def dispatch(i, c):
        o = n - 1 - i
        d = partner(o)
        disp[d] = gathered(pick(d), xi)
        dispatch_copy(o).start()
        return c

    lax.fori_loop(0, n - 1, dispatch, 0)

    for k in range(nt):
        small_out[k, 0:1, 0:rows] = cotangent[0:1, k * rows:(k + 1) * rows]
        small_out[k, 1:2, 0:ft] = tower_out[0:1, :]

    def small_copy(o, arriving=False):
        k = (ti + o) % nt
        return pltpu.make_async_remote_copy(
            src_ref=small_out.at[k], dst_ref=small_in.at[k if arriving else ti],
            send_sem=s_send.at[k], recv_sem=s_recv.at[k if arriving else ti],
            device_id={"task": k}, device_id_type=MESH)

    def send_small(o, c):
        small_copy(o).start()
        return c

    lax.fori_loop(1, nt, send_small, 0)
    small_in[ti] = small_out[ti]

    own = pick(zi)
    for j in range(m):
        held[zi, j] = gathered(own, j)
    zsum[...] = jnp.zeros_like(zsum)
    w_load.wait()
    tw_load.wait()

    def rs_copy(s, o, arriving=False):
        j = (xi + o) % m
        return pltpu.make_async_remote_copy(
            src_ref=rs_out.at[s, j], dst_ref=rs_in.at[s, j if arriving else xi],
            send_sem=rs_send.at[s, j], recv_sem=rs_recv.at[s, j if arriving else xi],
            device_id={"mp": j}, device_id_type=MESH)

    def expert(s):
        step = 512 if units % 512 == 0 else units
        for c0 in range(0, units, step):
            acc = jnp.zeros((slots, step), F32)
            for j in range(m):
                acc += jnp.dot(
                    held[s, j], w[j * depth:(j + 1) * depth, c0:c0 + step],
                    preferred_element_type=F32)
            hid[:, c0:c0 + step] = (acc * sigmoid(acc)).astype(BF16)
        for t in range(nt):
            u = jnp.dot(hid[...], tw[t], preferred_element_type=F32)
            c0 = (t % tl) * ft
            rs_out[s, t // tl, :, c0:c0 + ft] = u.astype(BF16)
        for o in range(1, m):
            rs_copy(s, o).start()

    def reduced(s):
        total = rs_out[s, xi].astype(F32)
        for o in range(1, m):
            rs_copy(s, o, True).wait_recv()
            total += rs_in[s, (xi + o) % m].astype(F32)
        return total.astype(BF16)

    def back_copy(s, arriving=False):
        return pltpu.make_async_remote_copy(
            src_ref=back_out.at[s], dst_ref=back_in.at[s if arriving else zi],
            send_sem=b_send.at[s], recv_sem=b_recv.at[s if arriving else zi],
            device_id={"dp": s}, device_id_type=MESH)

    def forward_copy(s, o, arriving=False):
        j = (xi + o) % m
        at = j if arriving else xi
        return pltpu.make_async_remote_copy(
            src_ref=held.at[s, at], dst_ref=held.at[s, at],
            send_sem=x_send.at[s, j], recv_sem=x_recv.at[s, at],
            device_id={"mp": j}, device_id_type=MESH)

    def arrive(s):
        pltpu.make_async_remote_copy(
            src_ref=disp.at[s], dst_ref=held.at[s, xi], send_sem=z_send.at[s],
            recv_sem=z_recv.at[s], device_id={"dp": s}, device_id_type=MESH).wait_recv()
        for o in range(1, m):
            forward_copy(s, o).start()

    def send_back(s):
        back_out[s] = reduced(s)
        back_copy(s).start()

    expert(zi)

    def work(o, c):
        s = partner(o)
        arrive(s)

        @pl.when(o > 1)
        def _():
            send_back(partner(o - 1))

        for p in range(1, m):
            forward_copy(s, p, True).wait_recv()
        expert(s)
        return c

    lax.fori_loop(1, n, work, 0)
    zsum[...] += jnp.dot(gate[zi], reduced(zi), preferred_element_type=F32)
    send_back(partner(n - 1))

    def collect(o, c):
        s = partner(o)
        back_copy(s, True).wait_recv()
        zsum[...] += jnp.dot(gate[s], back_in[s], preferred_element_type=F32)
        return c

    lax.fori_loop(1, n, collect, 0)

    def small_arrive(o, c):
        small_copy(o, True).wait_recv()
        return c

    lax.fori_loop(1, nt, small_arrive, 0)

    diagonal = (
        lax.broadcasted_iota(jnp.int32, (rows, rows), 0)
        == lax.broadcasted_iota(jnp.int32, (rows, rows), 1))

    def pred_copy(l, o):
        y = (xi + o) % m
        return pltpu.make_async_remote_copy(
            src_ref=pred_send.at[l], dst_ref=pred_in.at[ti], send_sem=p_send.at[l, o],
            recv_sem=p_recv.at[ti], device_id={"task": xi * tl + l, "mp": y},
            device_id_type=MESH)

    for l in range(tl):
        t = xi * tl + l
        z = zsum[:, l * ft:(l + 1) * ft] * scale
        s = sigmoid(z)
        out_row = small_in[t, 1:2, 0:ft]
        cot = jnp.sum(jnp.where(diagonal, small_in[t, 0:1, 0:rows], 0.0), axis=1, keepdims=True)
        dz[t] = (cot * out_row * s * (1.0 + z * (1.0 - s))).astype(BF16)
        pred = jnp.sum(z * s * out_row, axis=1, keepdims=True)
        pred_send[l, 0:1, 0:rows] = jnp.sum(jnp.where(diagonal, pred, 0.0), axis=0, keepdims=True)

    def dz_copy(o, arriving=False):
        j = (xi + o) % m
        at = pl.ds((j if arriving else xi) * tl, tl)
        return pltpu.make_async_remote_copy(
            src_ref=dz.at[at], dst_ref=dz.at[at], send_sem=d_send.at[j],
            recv_sem=d_recv.at[j if arriving else xi], device_id={"mp": j}, device_id_type=MESH)

    for o in range(1, m):
        dz_copy(o).start()
    for l in range(tl):
        mine = ti == xi * tl + l

        @pl.when(mine)
        def _():
            pred_in[ti] = pred_send[l]

        @pl.when(jnp.logical_not(mine))
        def _():
            pred_copy(l, 0).start()

        for o in range(1, m):
            pred_copy(l, o).start()

    for o in range(1, m):
        dz_copy(o, True).wait_recv()
    step = 512 if units % 512 == 0 else units
    for c0 in range(0, units, step):
        acc = jnp.zeros((rows, step), F32)
        for t in range(nt):
            acc += lax.dot_general(
                dz[t], tw[t, c0:c0 + step, :], (((1,), (1,)), ((), ())),
                preferred_element_type=F32)
        grad_out[:, c0:c0 + step] = acc.astype(BF16)

    keeper = ti // tl
    for k in range(nt):
        @pl.when(jnp.logical_not(jnp.logical_and(keeper == xi, ti == k)))
        def _():
            pltpu.make_async_remote_copy(
                src_ref=pred_send.at[0], dst_ref=pred_in.at[k], send_sem=p_send.at[0, 0],
                recv_sem=p_recv.at[k], device_id={"task": (ti + 1) % nt},
                device_id_type=MESH).wait_recv()

        pred_out[0:1, k * rows:(k + 1) * rows] = pred_in[k, 0:1, 0:rows]

    def drain(o, c):
        s = partner(o)
        dispatch_copy(o).wait_send()
        back_copy(s).wait_send()
        for p in range(1, m):
            forward_copy(s, p).wait_send()
            rs_copy(s, p).wait_send()
        return c

    lax.fori_loop(1, n, drain, 0)
    for p in range(1, m):
        rs_copy(zi, p).wait_send()
        dz_copy(p).wait_send()

    def drain_small(o, c):
        small_copy(o).wait_send()
        return c

    lax.fori_loop(1, nt, drain_small, 0)
    for l in range(tl):
        @pl.when(ti != xi * tl + l)
        def _():
            pred_copy(l, 0).wait_send()

        for o in range(1, m):
            pred_copy(l, o).wait_send()


def body(tokens, expert_ids, gate_levels, expert_weight, tower_weight, tower_out, cotangent):
    n, nt, m = lax.axis_size("dp"), lax.axis_size("task"), lax.axis_size("mp")
    rows, top = expert_ids.shape
    width, units = expert_weight.shape[1:]
    ft = tower_weight.shape[2]
    slots = -(-(5 * rows * top // (4 * n)) // 16) * 16
    depth = width // m
    tl = nt // m
    ucols = tl * ft
    wide = -(-max(rows, ft) // 128) * 128
    vmem = pl.BlockSpec(memory_space=pltpu.VMEM)
    hbm = pl.BlockSpec(memory_space=pl.ANY)
    dma = pltpu.SemaphoreType.DMA
    return tuple(pl.pallas_call(
        functools.partial(kernel, n, nt, m),
        out_shape=(
            jax.ShapeDtypeStruct((1, nt * rows), F32),
            jax.ShapeDtypeStruct((rows, units), BF16),
        ),
        in_specs=[hbm, vmem, vmem, hbm, hbm, vmem, vmem],
        out_specs=(vmem, vmem),
        scratch_shapes=[
            pltpu.VMEM((m, rows, depth), BF16),
            pltpu.VMEM((width, units), BF16),
            pltpu.VMEM(tower_weight.shape, BF16),
            pltpu.VMEM((n, slots, depth), BF16),
            pltpu.VMEM((n, m, slots, depth), BF16),
            pltpu.VMEM((n, rows, slots), BF16),
            pltpu.VMEM((slots, units), BF16),
            pltpu.VMEM((8, 128), F32),
            pltpu.VMEM((n, m, slots, ucols), BF16),
            pltpu.VMEM((n, m, slots, ucols), BF16),
            pltpu.VMEM((n, slots, ucols), BF16),
            pltpu.VMEM((n, slots, ucols), BF16),
            pltpu.VMEM((rows, ucols), F32),
            pltpu.VMEM((nt, rows, ft), BF16),
            pltpu.VMEM((nt, 8, wide), F32),
            pltpu.VMEM((nt, 8, wide), F32),
            pltpu.VMEM((tl, 8, wide), F32),
            pltpu.VMEM((nt, 8, wide), F32),
            dma((2 + m,)),
            dma((n,)), dma((n,)),
            dma((n, m)), dma((n, m)),
            dma((n, m)), dma((n, m)),
            dma((n,)), dma((n,)),
            dma((nt,)), dma((nt,)),
            dma((m,)), dma((m,)),
            dma((tl, m)), dma((nt,)),
        ],
        compiler_params=pltpu.CompilerParams(
            collective_id=0, has_side_effects=True, vmem_limit_bytes=48 * 1024 * 1024),
        name="expert_towers",
    )(tokens, expert_ids, gate_levels, expert_weight, tower_weight, tower_out, cotangent))


def solution(mesh):
    return jax.shard_map(
        body,
        mesh=mesh,
        in_specs=(
            P(("dp", "task"), None),
            P(("dp", "task"), None),
            P(("dp", "task"), None),
            P("dp", None, "mp"),
            P(None, "mp", None),
            P("task", None),
            P("task", "dp"),
        ),
        out_specs=(P("task", "dp"), P(("dp", "task"), "mp")),
        check_vma=False,
    )
```

time: 251 us -> 78 us (0.31)
  the two profiles are of different devices: /device:TPU:0 before, /device:TPU:10 now
where the time goes in v1:
time: 78 us; the launch traced here: 77.8 us
  Pallas kernels  69.4 us (89%)
  local copies, waits for them, and re-layouts  7.73 us (10%)
    pallas_call x1, Pallas kernels, body(): pl.pallas_call(functools.partial(kernel, n, nt, m), out_shape=(jax.ShapeD...  69.4 us
    unnamed x12, local copies, waits for them, and re-layouts  7.73 us

profile of v1, /device:TPU:10, one launch (start us, length us, event | category | flops | bytes accessed | tf_op | source)
XLA Modules:
  0.0 77.8 jit_solution(2992047025789756601)
XLA Ops:
  0.6 0.8 %copy.9.ids = s32[192,2]{1,0:T(8,128)S(1)} copy(s32[192,2]{0,1:T(2,128)} %param.8) | data formatting | bytes 3072 | tf_op args[1]
  1.4 0.8 %copy.10.levels = s32[192,2]{1,0:T(8,128)S(1)} copy(s32[192,2]{0,1:T(2,128)} %param.9) | data formatting | bytes 3072 | tf_op args[2]
  2.2 0.0 copy-start
  2.2 2.2 %copy-done = bf16[4,2048,256]{2,1,0:T(8,128)(2,1)S(1)} copy-done((bf16[4,2048,256]{2,1,0:T(8,128)(2,1)S(1)}, bf16[4,2048,256]{2,1,0:T(8,128)(2,1)}, u32[]{:S(2)}) %copy-start) | copy-done | bytes 4194328
  4.4 0.0 copy-start.1
  4.4 1.1 %copy-done.1 = bf16[192,2048]{1,0:T(8,128)(2,1)S(1)} copy-done((bf16[192,2048]{1,0:T(8,128)(2,1)S(1)}, bf16[192,2048]{1,0:T(8,128)(2,1)}, u32[]{:S(2)}) %copy-start.1) | copy-done | bytes 786456
  5.6 0.0 copy-start.2
  5.6 0.7 copy-done.2
  6.2 0.0 copy-start.3
  6.2 0.7 copy-done.3
  6.9 69.4 %expert_towers.1 = (f32[1,768]{1,0:T(1,128)S(1)}, bf16[192,2048]{1,0:T(8,128)(2,1)S(1)}) custom-call(bf16[192,2048]{1,0:T(8,128)(2,1)S(1)} %copy-done.1, s32[192,2]{1,0:T(8,128)S(1)} %copy.9.ids, s32[192,2]{1,0:T(8,128)S(1)} %copy.10.levels, bf16[1,2048,2048]{2,1,0:T(8,128)(2,1)} %weight.1, bf16[4,2048,256]{2,1,0:T(8,128)(2,1)S(1)} %copy-done, ...), custom_call_target="tpu_custom_call" | custom-call | tf_op jit(solution)/shard_map/expert_towers/pallas_call | solution.py:332
  76.3 0.6 copy.13
  76.9 0.9 %copy.14 = bf16[192,2048]{1,0:T(8,128)(2,1)} copy(bf16[192,2048]{1,0:T(8,128)(2,1)S(1)} %get-tuple-element.5) | data formatting | bytes 1572864
Async XLA Ops:
  2.2 2.2 %copy-start = (bf16[4,2048,256]{2,1,0:T(8,128)(2,1)S(1)}, bf16[4,2048,256]{2,1,0:T(8,128)(2,1)}, u32[]{:S(2)}) copy-start(bf16[4,2048,256]{2,1,0:T(8,128)(2,1)} %towers.1) | copy-start | bytes 12582916
  4.4 1.1 %copy-start.1 = (bf16[192,2048]{1,0:T(8,128)(2,1)S(1)}, bf16[192,2048]{1,0:T(8,128)(2,1)}, u32[]{:S(2)}) copy-start(bf16[192,2048]{1,0:T(8,128)(2,1)} %tokens.1) | copy-start | bytes 2359300
  5.6 0.7 copy-start.2
  6.2 0.7 copy-start.3

commit v2 on v1

v2 whole, which is shorter than its diff:
```python
import functools

import jax
import jax.numpy as jnp
from jax import lax
from jax.experimental import pallas as pl
from jax.experimental.pallas import tpu as pltpu
from jax.sharding import PartitionSpec as P

MESH = pl.DeviceIdType.MESH
F32 = jnp.float32
BF16 = jnp.bfloat16


def sigmoid(v):
    return 0.5 + 0.5 * jnp.tanh(0.5 * v)


def kernel(
    n, nt, m,
    tokens, ids_in, levels_in, weight, towers, tower_out_in, cotangent_in,
    pred_out, grad_out,
    tok, w, tw, ids, levels, tower_out, cotangent,
    disp, held, gate, pre, hid, part, rs_out, rs_in, back_out, back_in,
    zsum, dz, gsum, small_out, small_in, pred_send, pred_in,
    load_sem, z_send, z_recv, x_send, x_recv, rs_send, rs_recv, b_send, b_recv,
    s_send, s_recv, d_send, d_recv, p_send, p_recv,
):
    zi, ti, xi = lax.axis_index("dp"), lax.axis_index("task"), lax.axis_index("mp")
    rows = ids.shape[1]
    slots = gate.shape[2]
    chunks, _, depth = tok.shape
    each = chunks // m
    units = w.shape[1]
    ft = towers.shape[2]
    tl = nt // m
    step = 512 if units % 512 == 0 else units

    def partner(o):
        other, bit = 0, 1
        while bit < n:
            other = other + bit * ((zi // bit + o // bit) % 2)
            bit *= 2
        return other

    def load(src, dst, i):
        copy = pltpu.make_async_copy(src, dst, load_sem.at[i])
        copy.start()
        return copy

    routing = [load(ids_in, ids, 0), load(levels_in, levels, 1)]
    tok_loads = [
        load(tokens.at[:, pl.ds(c * depth, depth)], tok.at[c], 6 + c) for c in range(chunks)]
    small_loads = [load(tower_out_in, tower_out, 2), load(cotangent_in, cotangent, 3)]
    w_load = load(weight.at[0], w, 4)
    tw_load = load(towers, tw, 5)

    barrier = pltpu.get_barrier_semaphore()

    def greet_line(o, c):
        pl.semaphore_signal(barrier, inc=1, device_id={"dp": partner(o)}, device_id_type=MESH)
        return c

    def greet_plane(o, c):
        at = (ti * m + xi + o) % (nt * m)
        pl.semaphore_signal(
            barrier, inc=1, device_id={"task": at // m, "mp": at % m}, device_id_type=MESH)
        return c

    lax.fori_loop(1, n, greet_line, 0)
    lax.fori_loop(1, nt * m, greet_plane, 0)

    for copy in routing:
        copy.wait()
    names = max(8, n)
    sub = lax.broadcasted_iota(jnp.int32, (names, rows), 0)
    level_of = (
        jnp.where(ids[0:1, :] == sub, levels[0:1, :], 0)
        + jnp.where(ids[1:2, :] == sub, levels[1:2, :], 0)).astype(F32)
    named = jnp.where(level_of > 0, 1.0, 0.0)
    down = lax.broadcasted_iota(jnp.int32, (rows, rows), 0)
    across = lax.broadcasted_iota(jnp.int32, (rows, rows), 1)
    diagonal = down == across
    before = jnp.where(down < across, 1.0, 0.0)
    rank = jnp.dot(named.astype(BF16), before.astype(BF16), preferred_element_type=F32)
    place = jnp.where(named > 0, rank, -1.0)

    def row_of(table, d):
        return jnp.sum(jnp.where(sub == d, table, 0.0), axis=0, keepdims=True)

    def column(row):
        return jnp.sum(jnp.where(diagonal, row, 0.0), axis=1, keepdims=True)

    slot_down = lax.broadcasted_iota(jnp.int32, (slots, rows), 0).astype(F32)
    slot_across = lax.broadcasted_iota(jnp.int32, (rows, slots), 1).astype(F32)

    def pick(d):
        return jnp.where(slot_down == row_of(place, d), 1.0, 0.0).astype(BF16)

    def gathered(spot, c):
        return jnp.dot(spot, tok[c], preferred_element_type=F32).astype(BF16)

    for copy in tok_loads:
        copy.wait()

    def dispatch_copy(o, c, arriving=False):
        d = partner(o)
        return pltpu.make_async_remote_copy(
            src_ref=disp.at[d, c], dst_ref=held.at[d if arriving else zi, c],
            send_sem=z_send.at[d, c], recv_sem=z_recv.at[d if arriving else zi, c],
            device_id={"dp": d}, device_id_type=MESH)

    def fill(o, first, count):
        d = partner(o)
        spot = pick(d)
        for q in range(count):
            disp[d, first + q] = gathered(spot, first + q)

    fill(2, xi * each, each)
    pl.semaphore_wait(barrier, n - 1 + nt * m - 1)
    for q in range(each):
        dispatch_copy(2, xi * each + q).start()
    fill(1, 0, chunks)
    for c in range(chunks):
        dispatch_copy(1, c).start()

    def fill_rest(o, c):
        fill(o, xi * each, each)
        return c

    lax.fori_loop(3, n, fill_rest, 0)

    for copy in small_loads:
        copy.wait()
    for k in range(nt):
        small_out[k, 0:1, 0:rows] = cotangent[0:1, k * rows:(k + 1) * rows]
        small_out[k, 1:2, 0:ft] = tower_out[0:1, :]

    def small_copy(o, arriving=False):
        k = (ti + o) % nt
        return pltpu.make_async_remote_copy(
            src_ref=small_out.at[k], dst_ref=small_in.at[k if arriving else ti],
            send_sem=s_send.at[k], recv_sem=s_recv.at[k if arriving else ti],
            device_id={"task": k}, device_id_type=MESH)

    def send_small(o, c):
        small_copy(o).start()
        return c

    lax.fori_loop(1, nt, send_small, 0)
    small_in[ti] = small_out[ti]

    own = pick(zi)
    for c in range(chunks):
        held[zi, c] = gathered(own, c)

    def set_gate(d, c):
        hit = slot_across == column(row_of(place, d))
        gate[d] = jnp.where(hit, column(row_of(level_of, d)), 0.0).astype(BF16)
        return c

    lax.fori_loop(0, n, set_gate, 0)
    scale = 1.0 / column(jnp.sum(level_of, axis=0, keepdims=True))
    zsum[...] = jnp.zeros_like(zsum)
    w_load.wait()
    tw_load.wait()

    def rs_copy(s, o, arriving=False):
        j = (xi + o) % m
        return pltpu.make_async_remote_copy(
            src_ref=rs_out.at[s, j], dst_ref=rs_in.at[s, j if arriving else xi],
            send_sem=rs_send.at[s, j], recv_sem=rs_recv.at[s, j if arriving else xi],
            device_id={"mp": j}, device_id_type=MESH)

    def partial_pre(s, first, count, c0):
        acc = jnp.zeros((slots, step), F32)
        for q in range(count):
            at = first + q
            acc += jnp.dot(
                held[s, at], w[pl.ds(pl.multiple_of(at * depth, depth), depth), c0:c0 + step],
                preferred_element_type=F32)
        return acc

    def activate(acc, c0):
        hid[:, c0:c0 + step] = (acc * sigmoid(acc)).astype(BF16)

    def expert_whole(s):
        for c0 in range(0, units, step):
            activate(partial_pre(s, 0, chunks, c0), c0)

    def expert_own_columns(s):
        for c0 in range(0, units, step):
            pre[:, c0:c0 + step] = partial_pre(s, xi * each, each, c0)

    def expert_other_columns(s):
        for o in range(1, m):
            for q in range(each):
                forward_copy(s, o, q, True).wait_recv()
        for c0 in range(0, units, step):
            acc = pre[:, c0:c0 + step]
            for o in range(1, m):
                acc += partial_pre(s, (xi + o) % m * each, each, c0)
            activate(acc, c0)

    def tower_sums(s):
        for o in list(range(1, m)) + [0]:
            j = (xi + o) % m
            for l in range(tl):
                u = jnp.dot(hid[...], tw[j * tl + l], preferred_element_type=F32)
                if o == 0:
                    part[s, :, l * ft:(l + 1) * ft] = u
                else:
                    rs_out[s, j, :, l * ft:(l + 1) * ft] = u.astype(BF16)
            if o > 0:
                rs_copy(s, o).start()

    def reduced(s):
        total = part[s]
        for o in range(1, m):
            rs_copy(s, o, True).wait_recv()
            total += rs_in[s, (xi + o) % m].astype(F32)
        return total.astype(BF16)

    def back_copy(s, arriving=False):
        return pltpu.make_async_remote_copy(
            src_ref=back_out.at[s], dst_ref=back_in.at[s if arriving else zi],
            send_sem=b_send.at[s], recv_sem=b_recv.at[s if arriving else zi],
            device_id={"dp": s}, device_id_type=MESH)

    def forward_copy(s, o, q, arriving=False):
        j = (xi + o) % m
        at = (j if arriving else xi) * each + q
        return pltpu.make_async_remote_copy(
            src_ref=held.at[s, at], dst_ref=held.at[s, at],
            send_sem=x_send.at[s, j, q], recv_sem=x_recv.at[s, at],
            device_id={"mp": j}, device_id_type=MESH)

    def arrive(o):
        for q in range(each):
            dispatch_copy(o, xi * each + q, True).wait_recv()
            for p in range(1, m):
                forward_copy(partner(o), p, q).start()

    def send_back(s):
        back_out[s] = reduced(s)
        back_copy(s).start()

    expert_whole(zi)
    tower_sums(zi)

    def work(o, c):
        s = partner(o)
        for q in range(each):
            dispatch_copy(o, xi * each + q).wait_send()
            dispatch_copy(o + 1, xi * each + q).start()
        arrive(o)

        @pl.when(o > 2)
        def _():
            send_back(partner(o - 1))

        expert_own_columns(s)
        expert_other_columns(s)
        tower_sums(s)
        return c

    lax.fori_loop(2, n - 1, work, 0)
    near, last = partner(1), partner(n - 1)
    arrive(n - 1)
    send_back(partner(n - 2))
    for c in range(chunks):
        dispatch_copy(1, c, True).wait_recv()
    expert_whole(near)
    tower_sums(near)
    expert_own_columns(last)
    send_back(near)
    expert_other_columns(last)
    tower_sums(last)
    zsum[...] += jnp.dot(gate[zi], reduced(zi), preferred_element_type=F32)
    send_back(last)

    def collect(s):
        back_copy(s, True).wait_recv()
        zsum[...] += jnp.dot(gate[s], back_in[s], preferred_element_type=F32)

    def collect_step(o, c):
        collect(partner(o))
        return c

    lax.fori_loop(2, n - 1, collect_step, 0)
    collect(near)

    def small_arrive(o, c):
        small_copy(o, True).wait_recv()
        return c

    lax.fori_loop(1, nt, small_arrive, 0)
    cots = [column(small_in[xi * tl + l, 0:1, 0:rows]) for l in range(tl)]
    collect(last)

    def pred_copy(l, o):
        y = (xi + o) % m
        return pltpu.make_async_remote_copy(
            src_ref=pred_send.at[l], dst_ref=pred_in.at[ti], send_sem=p_send.at[l, o],
            recv_sem=p_recv.at[ti], device_id={"task": xi * tl + l, "mp": y},
            device_id_type=MESH)

    def dz_copy(l, o, arriving=False):
        j = (xi + o) % m
        at = (j if arriving else xi) * tl + l
        return pltpu.make_async_remote_copy(
            src_ref=dz.at[at], dst_ref=dz.at[at], send_sem=d_send.at[j, l],
            recv_sem=d_recv.at[at], device_id={"mp": j}, device_id_type=MESH)

    for l in range(tl):
        t = xi * tl + l
        z = zsum[:, l * ft:(l + 1) * ft] * scale
        s = sigmoid(z)
        out_row = small_in[t, 1:2, 0:ft]
        dz[t] = (cots[l] * out_row * s * (1.0 + z * (1.0 - s))).astype(BF16)
        for o in range(1, m):
            dz_copy(l, o).start()
        pred = jnp.sum(z * s * out_row, axis=1, keepdims=True)
        pred_send[l, 0:1, 0:rows] = jnp.sum(jnp.where(diagonal, pred, 0.0), axis=0, keepdims=True)
        mine = ti == t

        @pl.when(mine)
        def _():
            pred_in[ti] = pred_send[l]

        @pl.when(jnp.logical_not(mine))
        def _():
            pred_copy(l, 0).start()

        for o in range(1, m):
            pred_copy(l, o).start()

    def grad(o, c0):
        acc = jnp.zeros((rows, step), F32)
        for l in range(tl):
            t = (xi + o) % m * tl + l
            acc += lax.dot_general(
                dz[t], tw[t, c0:c0 + step, :], (((1,), (1,)), ((), ())),
                preferred_element_type=F32)
        return acc

    for c0 in range(0, units, step):
        gsum[:, c0:c0 + step] = grad(0, c0)
    for o in range(1, m):
        for l in range(tl):
            dz_copy(l, o, True).wait_recv()
    for c0 in range(0, units, step):
        acc = gsum[:, c0:c0 + step]
        for o in range(1, m):
            acc += grad(o, c0)
        grad_out[:, c0:c0 + step] = acc.astype(BF16)

    keeper = ti // tl
    for k in range(nt):
        @pl.when(jnp.logical_not(jnp.logical_and(keeper == xi, ti == k)))
        def _():
            pltpu.make_async_remote_copy(
                src_ref=pred_send.at[0], dst_ref=pred_in.at[k], send_sem=p_send.at[0, 0],
                recv_sem=p_recv.at[k], device_id={"task": (ti + 1) % nt},
                device_id_type=MESH).wait_recv()

        pred_out[0:1, k * rows:(k + 1) * rows] = pred_in[k, 0:1, 0:rows]

    def drain(o, c):
        s = partner(o)
        back_copy(s).wait_send()
        for p in range(1, m):
            rs_copy(s, p).wait_send()
        return c

    def drain_far(o, c):
        for p in range(1, m):
            for q in range(each):
                forward_copy(partner(o), p, q).wait_send()
        return c

    lax.fori_loop(1, n, drain, 0)
    lax.fori_loop(2, n, drain_far, 0)
    for c in range(chunks):
        dispatch_copy(1, c).wait_send()
    for q in range(each):
        dispatch_copy(n - 1, xi * each + q).wait_send()
    for p in range(1, m):
        rs_copy(zi, p).wait_send()
        for l in range(tl):
            dz_copy(l, p).wait_send()

    def drain_small(o, c):
        small_copy(o).wait_send()
        return c

    lax.fori_loop(1, nt, drain_small, 0)
    for l in range(tl):
        @pl.when(ti != xi * tl + l)
        def _():
            pred_copy(l, 0).wait_send()

        for o in range(1, m):
            pred_copy(l, o).wait_send()


def body(tokens, expert_ids, gate_levels, expert_weight, tower_weight, tower_out, cotangent):
    n, nt, m = lax.axis_size("dp"), lax.axis_size("task"), lax.axis_size("mp")
    rows, top = expert_ids.shape
    width, units = expert_weight.shape[1:]
    ft = tower_weight.shape[2]
    slots = -(-(5 * rows * top // (4 * n)) // 16) * 16
    depth = width // m
    tl = nt // m
    ucols = tl * ft
    wide = -(-max(rows, ft) // 128) * 128
    each = 2
    chunks = m * each
    depth = width // chunks
    vmem = pl.BlockSpec(memory_space=pltpu.VMEM)
    hbm = pl.BlockSpec(memory_space=pltpu.HBM)
    dma = pltpu.SemaphoreType.DMA
    return tuple(pl.pallas_call(
        functools.partial(kernel, n, nt, m),
        out_shape=(
            jax.ShapeDtypeStruct((1, nt * rows), F32),
            jax.ShapeDtypeStruct((rows, units), BF16),
        ),
        in_specs=[hbm] * 7,
        out_specs=(vmem, vmem),
        scratch_shapes=[
            pltpu.VMEM((chunks, rows, depth), BF16),
            pltpu.VMEM((width, units), BF16),
            pltpu.VMEM(tower_weight.shape, BF16),
            pltpu.VMEM((top, rows), jnp.int32),
            pltpu.VMEM((top, rows), jnp.int32),
            pltpu.VMEM(tower_out.shape, F32),
            pltpu.VMEM(cotangent.shape, F32),
            pltpu.VMEM((n, chunks, slots, depth), BF16),
            pltpu.VMEM((n, chunks, slots, depth), BF16),
            pltpu.VMEM((n, rows, slots), BF16),
            pltpu.VMEM((slots, units), F32),
            pltpu.VMEM((slots, units), BF16),
            pltpu.VMEM((n, slots, ucols), F32),
            pltpu.VMEM((n, m, slots, ucols), BF16),
            pltpu.VMEM((n, m, slots, ucols), BF16),
            pltpu.VMEM((n, slots, ucols), BF16),
            pltpu.VMEM((n, slots, ucols), BF16),
            pltpu.VMEM((rows, ucols), F32),
            pltpu.VMEM((nt, rows, ft), BF16),
            pltpu.VMEM((rows, units), F32),
            pltpu.VMEM((nt, 8, wide), F32),
            pltpu.VMEM((nt, 8, wide), F32),
            pltpu.VMEM((tl, 8, wide), F32),
            pltpu.VMEM((nt, 8, wide), F32),
            dma((6 + chunks,)),
            dma((n, chunks)), dma((n, chunks)),
            dma((n, m, each)), dma((n, chunks)),
            dma((n, m)), dma((n, m)),
            dma((n,)), dma((n,)),
            dma((nt,)), dma((nt,)),
            dma((m, tl)), dma((nt,)),
            dma((tl, m)), dma((nt,)),
        ],
        compiler_params=pltpu.CompilerParams(
            collective_id=0, has_side_effects=True, vmem_limit_bytes=40 * 1024 * 1024),
        name="expert_towers",
    )(tokens, expert_ids.T, gate_levels.T, expert_weight, tower_weight, tower_out, cotangent))


def solution(mesh):
    return jax.shard_map(
        body,
        mesh=mesh,
        in_specs=(
            P(("dp", "task"), None),
            P(("dp", "task"), None),
            P(("dp", "task"), None),
            P("dp", None, "mp"),
            P(None, "mp", None),
            P("task", None),
            P("task", "dp"),
        ),
        out_specs=(P("task", "dp"), P(("dp", "task"), "mp")),
        check_vma=False,
    )
```

time: 78 us -> 68.2 us (0.87)
  the two profiles are of different devices: /device:TPU:10 before, /device:TPU:0 now
where the time goes in v2:
time: 68.2 us; the launch traced here: 67.9 us
  Pallas kernels  56.4 us (83%)
  local copies, waits for them, and re-layouts  10.9 us (16%)
    pallas_call x1, Pallas kernels, body(): pl.pallas_call(functools.partial(kernel, n, nt, m), out_shape=(jax.ShapeD...  56.4 us
    unnamed x16, local copies, waits for them, and re-layouts  10.9 us

profile of v2, /device:TPU:0, one launch (start us, length us, event | category | flops | bytes accessed | tf_op | source)
XLA Modules:
  0.0 67.9 jit_solution(16780715938422818881)
XLA Ops:
  0.6 0.0 copy-start
  0.6 3.4 %copy-done = bf16[1,2048,2048]{2,1,0:T(8,128)(2,1)S(1)} copy-done((bf16[1,2048,2048]{2,1,0:T(8,128)(2,1)S(1)}, bf16[1,2048,2048]{2,1,0:T(8,128)(2,1)}, u32[]{:S(2)}) %copy-start) | copy-done | bytes 8388632
  4.0 0.0 copy-start.1
  4.0 2.2 %copy-done.1 = bf16[4,2048,256]{2,1,0:T(8,128)(2,1)S(1)} copy-done((bf16[4,2048,256]{2,1,0:T(8,128)(2,1)S(1)}, bf16[4,2048,256]{2,1,0:T(8,128)(2,1)}, u32[]{:S(2)}) %copy-start.1) | copy-done | bytes 4194328
  6.2 0.0 copy-start.2
  6.2 1.1 %copy-done.2 = bf16[192,2048]{1,0:T(8,128)(2,1)S(1)} copy-done((bf16[192,2048]{1,0:T(8,128)(2,1)S(1)}, bf16[192,2048]{1,0:T(8,128)(2,1)}, u32[]{:S(2)}) %copy-start.2) | copy-done | bytes 786456
  7.3 0.0 copy-start.3
  7.3 0.7 %copy-done.3 = f32[1,768]{1,0:T(1,128)S(1)} copy-done((f32[1,768]{1,0:T(1,128)S(1)}, f32[1,768]{1,0:T(1,128)}, u32[]{:S(2)}) %copy-start.3) | copy-done | bytes 3096
  8.0 0.0 copy-start.4
  8.0 0.7 %copy-done.4 = s32[192,2]{0,1:T(2,128)S(1)} copy-done((s32[192,2]{0,1:T(2,128)S(1)}, s32[192,2]{0,1:T(2,128)}, u32[]{:S(2)}) %copy-start.4) | copy-done | bytes 1560
  8.7 0.0 copy-start.5
  8.7 0.7 %copy-done.5 = s32[192,2]{0,1:T(2,128)S(1)} copy-done((s32[192,2]{0,1:T(2,128)S(1)}, s32[192,2]{0,1:T(2,128)}, u32[]{:S(2)}) %copy-start.5) | copy-done | bytes 1560
  9.4 0.0 copy-start.6
  9.4 0.7 copy-done.6
  10.1 56.4 %expert_towers.1 = (f32[1,768]{1,0:T(1,128)S(1)}, bf16[192,2048]{1,0:T(8,128)(2,1)S(1)}) custom-call(bf16[192,2048]{1,0:T(8,128)(2,1)S(1)} %copy-done.2, s32[2,192]{1,0:T(2,128)S(1)} %bitcast.2, s32[2,192]{1,0:T(2,128)S(1)} %bitcast.3, bf16[1,2048,2048]{2,1,0:T(8,128)(2,1)S(1)} %copy-done, bf16[4,2048,256]{2,1,0:T(8,128)(2,1)S(1)} %copy-done.1, ...), custom_call_target="tpu_custom_call" | custom-call | tf_op jit(solution)/shard_map/expert_towers/pallas_call | solution.py:423
  66.4 0.6 copy.11
  67.0 0.9 %copy.12 = bf16[192,2048]{1,0:T(8,128)(2,1)} copy(bf16[192,2048]{1,0:T(8,128)(2,1)S(1)} %get-tuple-element.5) | data formatting | bytes 1572864
Async XLA Ops:
  0.6 3.4 %copy-start = (bf16[1,2048,2048]{2,1,0:T(8,128)(2,1)S(1)}, bf16[1,2048,2048]{2,1,0:T(8,128)(2,1)}, u32[]{:S(2)}) copy-start(bf16[1,2048,2048]{2,1,0:T(8,128)(2,1)} %weight.1) | copy-start | bytes 25165828
  4.0 2.2 %copy-start.1 = (bf16[4,2048,256]{2,1,0:T(8,128)(2,1)S(1)}, bf16[4,2048,256]{2,1,0:T(8,128)(2,1)}, u32[]{:S(2)}) copy-start(bf16[4,2048,256]{2,1,0:T(8,128)(2,1)} %towers.1) | copy-start | bytes 12582916
  6.2 1.1 %copy-start.2 = (bf16[192,2048]{1,0:T(8,128)(2,1)S(1)}, bf16[192,2048]{1,0:T(8,128)(2,1)}, u32[]{:S(2)}) copy-start(bf16[192,2048]{1,0:T(8,128)(2,1)} %tokens.1) | copy-start | bytes 2359300
  7.3 0.7 %copy-start.3 = (f32[1,768]{1,0:T(1,128)S(1)}, f32[1,768]{1,0:T(1,128)}, u32[]{:S(2)}) copy-start(f32[1,768]{1,0:T(1,128)} %cotangent_in.1) | copy-start | bytes 9220
  8.0 0.7 %copy-start.4 = (s32[192,2]{0,1:T(2,128)S(1)}, s32[192,2]{0,1:T(2,128)}, u32[]{:S(2)}) copy-start(s32[192,2]{0,1:T(2,128)} %param.8) | copy-start | bytes 4612
  8.7 0.7 %copy-start.5 = (s32[192,2]{0,1:T(2,128)S(1)}, s32[192,2]{0,1:T(2,128)}, u32[]{:S(2)}) copy-start(s32[192,2]{0,1:T(2,128)} %param.9) | copy-start | bytes 4612
  9.4 0.7 %copy-start.6 = (f32[1,256]{1,0:T(1,128)S(1)}, f32[1,256]{1,0:T(1,128)}, u32[]{:S(2)}) copy-start(f32[1,256]{1,0:T(1,128)} %tower_out_in.1) | copy-start | bytes 3076

commit v3 on v2

--- a/solution.py
+++ b/solution.py
@@ -22,9 +22,9 @@
     pred_out, grad_out,
     tok, w, tw, ids, levels, tower_out, cotangent,
     disp, held, gate, pre, hid, part, rs_out, rs_in, back_out, back_in,
-    zsum, dz, gsum, small_out, small_in, pred_send, pred_in,
+    zsum, dz, gsum, gout, pred, small_out, small_in, pred_send, pred_in,
     load_sem, z_send, z_recv, x_send, x_recv, rs_send, rs_recv, b_send, b_recv,
-    s_send, s_recv, d_send, d_recv, p_send, p_recv,
+    s_send, s_recv, d_send, d_recv, p_send, p_recv, out_sem,
 ):
     zi, ti, xi = lax.axis_index("dp"), lax.axis_index("task"), lax.axis_index("mp")
     rows = ids.shape[1]
@@ -165,11 +165,11 @@
     w_load.wait()
     tw_load.wait()
 
-    def rs_copy(s, o, arriving=False):
+    def rs_copy(s, o, l, arriving=False):
         j = (xi + o) % m
         return pltpu.make_async_remote_copy(
-            src_ref=rs_out.at[s, j], dst_ref=rs_in.at[s, j if arriving else xi],
-            send_sem=rs_send.at[s, j], recv_sem=rs_recv.at[s, j if arriving else xi],
+            src_ref=rs_out.at[s, j, l], dst_ref=rs_in.at[s, j if arriving else xi, l],
+            send_sem=rs_send.at[s, j, l], recv_sem=rs_recv.at[s, j if arriving else xi, l],
             device_id={"mp": j}, device_id_type=MESH)
 
     def partial_pre(s, first, count, c0):
@@ -203,28 +203,26 @@
             activate(acc, c0)
 
     def tower_sums(s):
-        for o in list(range(1, m)) + [0]:
-            j = (xi + o) % m
+        for o in range(1, m):
             for l in range(tl):
+                j = (xi + o) % m
                 u = jnp.dot(hid[...], tw[j * tl + l], preferred_element_type=F32)
-                if o == 0:
-                    part[s, :, l * ft:(l + 1) * ft] = u
-                else:
-                    rs_out[s, j, :, l * ft:(l + 1) * ft] = u.astype(BF16)
-            if o > 0:
-                rs_copy(s, o).start()
-
-    def reduced(s):
-        total = part[s]
-        for o in range(1, m):
-            rs_copy(s, o, True).wait_recv()
-            total += rs_in[s, (xi + o) % m].astype(F32)
+                rs_out[s, j, l] = u.astype(BF16)
+                rs_copy(s, o, l).start()
+        for l in range(tl):
+            part[s, l] = jnp.dot(hid[...], tw[xi * tl + l], preferred_element_type=F32)
+
+    def reduced(s, l):
+        total = part[s, l]
+        for o in range(1, m):
+            rs_copy(s, o, l, True).wait_recv()
+            total += rs_in[s, (xi + o) % m, l].astype(F32)
         return total.astype(BF16)
 
-    def back_copy(s, arriving=False):
-        return pltpu.make_async_remote_copy(
-            src_ref=back_out.at[s], dst_ref=back_in.at[s if arriving else zi],
-            send_sem=b_send.at[s], recv_sem=b_recv.at[s if arriving else zi],
+    def back_copy(s, l, arriving=False):
+        return pltpu.make_async_remote_copy(
+            src_ref=back_out.at[s, l], dst_ref=back_in.at[s if arriving else zi, l],
+            send_sem=b_send.at[s, l], recv_sem=b_recv.at[s if arriving else zi, l],
             device_id={"dp": s}, device_id_type=MESH)
 
     def forward_copy(s, o, q, arriving=False):
@@ -242,8 +240,9 @@
                 forward_copy(partner(o), p, q).start()
 
     def send_back(s):
-        back_out[s] = reduced(s)
-        back_copy(s).start()
+        for l in range(tl):
+            back_out[s, l] = reduced(s, l)
+            back_copy(s, l).start()
 
     expert_whole(zi)
     tower_sums(zi)
@@ -276,19 +275,18 @@
     send_back(near)
     expert_other_columns(last)
     tower_sums(last)
-    zsum[...] += jnp.dot(gate[zi], reduced(zi), preferred_element_type=F32)
     send_back(last)
-
-    def collect(s):
-        back_copy(s, True).wait_recv()
-        zsum[...] += jnp.dot(gate[s], back_in[s], preferred_element_type=F32)
+    for l in range(tl):
+        zsum[l] += jnp.dot(gate[zi], reduced(zi, l), preferred_element_type=F32)
+
+    def collect(s, l):
+        back_copy(s, l, True).wait_recv()
+        zsum[l] += jnp.dot(gate[s], back_in[s, l], preferred_element_type=F32)
 
     def collect_step(o, c):
-        collect(partner(o))
-        return c
-
-    lax.fori_loop(2, n - 1, collect_step, 0)
-    collect(near)
+        for l in range(tl):
+            collect(partner(o), l)
+        return c
 
     def small_arrive(o, c):
         small_copy(o, True).wait_recv()
@@ -296,7 +294,9 @@
 
     lax.fori_loop(1, nt, small_arrive, 0)
     cots = [column(small_in[xi * tl + l, 0:1, 0:rows]) for l in range(tl)]
-    collect(last)
+    lax.fori_loop(2, n - 1, collect_step, 0)
+    for l in range(tl):
+        collect(near, l)
 
     def pred_copy(l, o):
         y = (xi + o) % m
@@ -314,14 +314,15 @@
 
     for l in range(tl):
         t = xi * tl + l
-        z = zsum[:, l * ft:(l + 1) * ft] * scale
+        collect(last, l)
+        z = zsum[l] * scale
         s = sigmoid(z)
         out_row = small_in[t, 1:2, 0:ft]
         dz[t] = (cots[l] * out_row * s * (1.0 + z * (1.0 - s))).astype(BF16)
         for o in range(1, m):
             dz_copy(l, o).start()
-        pred = jnp.sum(z * s * out_row, axis=1, keepdims=True)
-        pred_send[l, 0:1, 0:rows] = jnp.sum(jnp.where(diagonal, pred, 0.0), axis=0, keepdims=True)
+        value = jnp.sum(z * s * out_row, axis=1, keepdims=True)
+        pred_send[l, 0:1, 0:rows] = jnp.sum(jnp.where(diagonal, value, 0.0), axis=0, keepdims=True)
         mine = ti == t
 
         @pl.when(mine)
@@ -349,11 +350,16 @@
     for o in range(1, m):
         for l in range(tl):
             dz_copy(l, o, True).wait_recv()
+    grad_writes = []
     for c0 in range(0, units, step):
         acc = gsum[:, c0:c0 + step]
         for o in range(1, m):
             acc += grad(o, c0)
-        grad_out[:, c0:c0 + step] = acc.astype(BF16)
+        block = c0 // step
+        gout[block] = acc.astype(BF16)
+        grad_writes.append(pltpu.make_async_copy(
+            gout.at[block], grad_out.at[:, pl.ds(c0, step)], out_sem.at[block]))
+        grad_writes[-1].start()
 
     keeper = ti // tl
     for k in range(nt):
@@ -364,13 +370,17 @@
                 recv_sem=p_recv.at[k], device_id={"task": (ti + 1) % nt},
                 device_id_type=MESH).wait_recv()
 
-        pred_out[0:1, k * rows:(k + 1) * rows] = pred_in[k, 0:1, 0:rows]
+        pred[0:1, k * rows:(k + 1) * rows] = pred_in[k, 0:1, 0:rows]
+
+    pred_write = pltpu.make_async_copy(pred, pred_out, out_sem.at[units // step])
+    pred_write.start()
 
     def drain(o, c):
         s = partner(o)
-        back_copy(s).wait_send()
-        for p in range(1, m):
-            rs_copy(s, p).wait_send()
+        for l in range(tl):
+            back_copy(s, l).wait_send()
+            for p in range(1, m):
+                rs_copy(s, p, l).wait_send()
         return c
 
     def drain_far(o, c):
@@ -386,8 +396,8 @@
     for q in range(each):
         dispatch_copy(n - 1, xi * each + q).wait_send()
     for p in range(1, m):
-        rs_copy(zi, p).wait_send()
-        for l in range(tl):
+        for l in range(tl):
+            rs_copy(zi, p, l).wait_send()
             dz_copy(l, p).wait_send()
 
     def drain_small(o, c):
@@ -402,6 +412,9 @@
 
         for o in range(1, m):
             pred_copy(l, o).wait_send()
+    for copy in grad_writes:
+        copy.wait()
+    pred_write.wait()
 
 
 def body(tokens, expert_ids, gate_levels, expert_weight, tower_weight, tower_out, cotangent):
@@ -412,12 +425,11 @@
     slots = -(-(5 * rows * top // (4 * n)) // 16) * 16
     depth = width // m
     tl = nt // m
-    ucols = tl * ft
+    step = 512 if units % 512 == 0 else units
     wide = -(-max(rows, ft) // 128) * 128
     each = 2
     chunks = m * each
     depth = width // chunks
-    vmem = pl.BlockSpec(memory_space=pltpu.VMEM)
     hbm = pl.BlockSpec(memory_space=pltpu.HBM)
     dma = pltpu.SemaphoreType.DMA
     return tuple(pl.pallas_call(
@@ -427,7 +439,7 @@
             jax.ShapeDtypeStruct((rows, units), BF16),
         ),
         in_specs=[hbm] * 7,
-        out_specs=(vmem, vmem),
+        out_specs=(hbm, hbm),
         scratch_shapes=[
             pltpu.VMEM((chunks, rows, depth), BF16),
             pltpu.VMEM((width, units), BF16),
@@ -441,14 +453,16 @@
             pltpu.VMEM((n, rows, slots), BF16),
             pltpu.VMEM((slots, units), F32),
             pltpu.VMEM((slots, units), BF16),
-            pltpu.VMEM((n, slots, ucols), F32),
-            pltpu.VMEM((n, m, slots, ucols), BF16),
-            pltpu.VMEM((n, m, slots, ucols), BF16),
-            pltpu.VMEM((n, slots, ucols), BF16),
-            pltpu.VMEM((n, slots, ucols), BF16),
-            pltpu.VMEM((rows, ucols), F32),
+            pltpu.VMEM((n, tl, slots, ft), F32),
+            pltpu.VMEM((n, m, tl, slots, ft), BF16),
+            pltpu.VMEM((n, m, tl, slots, ft), BF16),
+            pltpu.VMEM((n, tl, slots, ft), BF16),
+            pltpu.VMEM((n, tl, slots, ft), BF16),
+            pltpu.VMEM((tl, rows, ft), F32),
             pltpu.VMEM((nt, rows, ft), BF16),
             pltpu.VMEM((rows, units), F32),
+            pltpu.VMEM((units // step, rows, step), BF16),
+            pltpu.VMEM((1, nt * rows), F32),
             pltpu.VMEM((nt, 8, wide), F32),
             pltpu.VMEM((nt, 8, wide), F32),
             pltpu.VMEM((tl, 8, wide), F32),
@@ -456,14 +470,14 @@
             dma((6 + chunks,)),
             dma((n, chunks)), dma((n, chunks)),
             dma((n, m, each)), dma((n, chunks)),
-            dma((n, m)), dma((n, m)),
-            dma((n,)), dma((n,)),
+            dma((n, m, tl)), dma((n, m, tl)),
+            dma((n, tl)), dma((n, tl)),
             dma((nt,)), dma((nt,)),
             dma((m, tl)), dma((nt,)),
-            dma((tl, m)), dma((nt,)),
+            dma((tl, m)), dma((nt,)), dma((units // step + 1,)),
         ],
         compiler_params=pltpu.CompilerParams(
-            collective_id=0, has_side_effects=True, vmem_limit_bytes=40 * 1024 * 1024),
+            collective_id=0, has_side_effects=True, vmem_limit_bytes=60 * 1024 * 1024),
         name="expert_towers",
     )(tokens, expert_ids.T, gate_levels.T, expert_weight, tower_weight, tower_out, cotangent))
 

time: 68.2 us -> 58.9 us (0.86)
  local copies, waits for them, and re-layouts: 10.9 us -> 3.34 us
  Pallas kernels: 56.4 us -> 54.8 us
    unnamed x16 -> x2, local copies, waits for them, and re-layouts: 10.9 us -> 3.34 us
    pallas_call x1, Pallas kernels: 56.4 us -> 54.8 us  [body(): pl.pallas_call(functools.partial(kernel, n, nt, m), out_shape=(jax.ShapeD...]
where the time goes in v3:
time: 58.9 us; the launch traced here: 58.7 us
  Pallas kernels  54.8 us (93%)
  local copies, waits for them, and re-layouts  3.34 us (6%)
  between operations  0.64 us (1%)
    pallas_call x1, Pallas kernels, body(): pl.pallas_call(functools.partial(kernel, n, nt, m), out_shape=(jax.ShapeD...  54.8 us
    unnamed x2, local copies, waits for them, and re-layouts  3.34 us

profile of v3, /device:TPU:0, one launch (start us, length us, event | category | flops | bytes accessed | tf_op | source)
XLA Modules:
  0.0 58.7 jit_solution(6656448557572320884)
XLA Ops:
  0.6 54.8 %expert_towers.1 = (f32[1,768]{1,0:T(1,128)}, bf16[192,2048]{1,0:T(8,128)(2,1)}) custom-call(bf16[192,2048]{1,0:T(8,128)(2,1)} %tokens.1, s32[2,192]{1,0:T(2,128)} %bitcast.2, s32[2,192]{1,0:T(2,128)} %bitcast.3, bf16[1,2048,2048]{2,1,0:T(8,128)(2,1)} %weight.1, bf16[4,2048,256]{2,1,0:T(8,128)(2,1)} %towers.1, f32[1,256]{1,0:T(1,128)} %tower_out_in.1, ...), custom_call_target="tpu_custom_call" | custom-call | tf_op jit(solution)/shard_map/expert_towers/pallas_call | solution.py:435
  55.4 1.3 %copy.11 = f32[1,768]{1,0:T(1,128)} copy(f32[1,768]{1,0:T(1,128)} %get-tuple-element.4) | data formatting | bytes 6144
  56.7 2.1 %copy.12 = bf16[192,2048]{1,0:T(8,128)(2,1)} copy(bf16[192,2048]{1,0:T(8,128)(2,1)} %get-tuple-element.5) | data formatting | bytes 1572864

commit v4 on v3

--- a/solution.py
+++ b/solution.py
@@ -21,7 +21,7 @@
     tokens, ids_in, levels_in, weight, towers, tower_out_in, cotangent_in,
     pred_out, grad_out,
     tok, w, tw, ids, levels, tower_out, cotangent,
-    disp, held, gate, pre, hid, part, rs_out, rs_in, back_out, back_in,
+    disp, held, gate, pre, near_pre, hid, part, rs_out, rs_in, back_out, back_in,
     zsum, dz, gsum, gout, pred, small_out, small_in, pred_send, pred_in,
     load_sem, z_send, z_recv, x_send, x_recv, rs_send, rs_recv, b_send, b_recv,
     s_send, s_recv, d_send, d_recv, p_send, p_recv, out_sem,
@@ -172,35 +172,27 @@
             send_sem=rs_send.at[s, j, l], recv_sem=rs_recv.at[s, j if arriving else xi, l],
             device_id={"mp": j}, device_id_type=MESH)
 
-    def partial_pre(s, first, count, c0):
-        acc = jnp.zeros((slots, step), F32)
-        for q in range(count):
-            at = first + q
-            acc += jnp.dot(
-                held[s, at], w[pl.ds(pl.multiple_of(at * depth, depth), depth), c0:c0 + step],
-                preferred_element_type=F32)
-        return acc
-
-    def activate(acc, c0):
-        hid[:, c0:c0 + step] = (acc * sigmoid(acc)).astype(BF16)
-
-    def expert_whole(s):
+    def accumulate(sums, s, ats, fresh=False, finish=False):
         for c0 in range(0, units, step):
-            activate(partial_pre(s, 0, chunks, c0), c0)
-
-    def expert_own_columns(s):
-        for c0 in range(0, units, step):
-            pre[:, c0:c0 + step] = partial_pre(s, xi * each, each, c0)
-
-    def expert_other_columns(s):
-        for o in range(1, m):
-            for q in range(each):
-                forward_copy(s, o, q, True).wait_recv()
-        for c0 in range(0, units, step):
-            acc = pre[:, c0:c0 + step]
-            for o in range(1, m):
-                acc += partial_pre(s, (xi + o) % m * each, each, c0)
-            activate(acc, c0)
+            acc = jnp.zeros((slots, step), F32) if fresh else sums[:, c0:c0 + step]
+            for at in ats:
+                acc += jnp.dot(
+                    held[s, at], w[pl.ds(pl.multiple_of(at * depth, depth), depth), c0:c0 + step],
+                    preferred_element_type=F32)
+            if finish:
+                hid[:, c0:c0 + step] = (acc * sigmoid(acc)).astype(BF16)
+            else:
+                sums[:, c0:c0 + step] = acc
+
+    def own_chunk(q):
+        return xi * each + q
+
+    def other_chunks(q):
+        return [(xi + o) % m * each + q for o in range(1, m)]
+
+    def wait_others(s, q):
+        for o in range(1, m):
+            forward_copy(s, o, q, True).wait_recv()
 
     def tower_sums(s):
         for o in range(1, m):
@@ -233,47 +225,68 @@
             send_sem=x_send.at[s, j, q], recv_sem=x_recv.at[s, at],
             device_id={"mp": j}, device_id_type=MESH)
 
-    def arrive(o):
-        for q in range(each):
-            dispatch_copy(o, xi * each + q, True).wait_recv()
-            for p in range(1, m):
-                forward_copy(partner(o), p, q).start()
+    def forward(o, q):
+        dispatch_copy(o, own_chunk(q), True).wait_recv()
+        for p in range(1, m):
+            forward_copy(partner(o), p, q).start()
 
     def send_back(s):
         for l in range(tl):
             back_out[s, l] = reduced(s, l)
             back_copy(s, l).start()
 
-    expert_whole(zi)
+    accumulate(pre, zi, range(chunks), fresh=True, finish=True)
     tower_sums(zi)
 
     def work(o, c):
         s = partner(o)
         for q in range(each):
-            dispatch_copy(o, xi * each + q).wait_send()
-            dispatch_copy(o + 1, xi * each + q).start()
-        arrive(o)
+            dispatch_copy(o, own_chunk(q)).wait_send()
+            dispatch_copy(o + 1, own_chunk(q)).start()
+        for q in range(each):
+            forward(o, q)
 
         @pl.when(o > 2)
         def _():
             send_back(partner(o - 1))
 
-        expert_own_columns(s)
-        expert_other_columns(s)
+        accumulate(pre, s, [own_chunk(q) for q in range(each)], fresh=True)
+        for q in range(each):
+            wait_others(s, q)
+        accumulate(
+            pre, s, [at for q in range(each) for at in other_chunks(q)], finish=True)
         tower_sums(s)
         return c
 
     lax.fori_loop(2, n - 1, work, 0)
+
     near, last = partner(1), partner(n - 1)
-    arrive(n - 1)
+    cuts = (0, chunks // 2, 3 * chunks // 4, chunks)
+
+    def near_group(g):
+        ats = range(cuts[g], cuts[g + 1])
+        for at in ats:
+            dispatch_copy(1, at, True).wait_recv()
+        accumulate(near_pre, near, ats, fresh=g == 0, finish=g == 2)
+
+    forward(n - 1, 0)
+    forward(n - 1, 1)
     send_back(partner(n - 2))
-    for c in range(chunks):
-        dispatch_copy(1, c, True).wait_recv()
-    expert_whole(near)
+    near_group(0)
+    forward(n - 1, 2)
+    wait_others(last, 0)
+    accumulate(pre, last, [own_chunk(0), own_chunk(1)] + other_chunks(0), fresh=True)
+    near_group(1)
+    forward(n - 1, 3)
+    near_group(2)
     tower_sums(near)
-    expert_own_columns(last)
+    wait_others(last, 1)
+    wait_others(last, 2)
+    accumulate(
+        pre, last, [own_chunk(2), own_chunk(3)] + other_chunks(1) + other_chunks(2))
     send_back(near)
-    expert_other_columns(last)
+    wait_others(last, 3)
+    accumulate(pre, last, other_chunks(3), finish=True)
     tower_sums(last)
     send_back(last)
     for l in range(tl):
@@ -415,6 +428,18 @@
     for copy in grad_writes:
         copy.wait()
     pred_write.wait()
+
+
+def hand_over(pred, grad, pred_out, grad_out, sem):
+    rows = grad.shape[0] // 4
+    copies = [pltpu.make_async_copy(pred, pred_out, sem.at[4])]
+    for i in range(4):
+        at = pl.ds(i * rows, rows)
+        copies.append(pltpu.make_async_copy(grad.at[at, :], grad_out.at[at, :], sem.at[i]))
+    for copy in copies:
+        copy.start()
+    for copy in copies:
+        copy.wait()
 
 
 def body(tokens, expert_ids, gate_levels, expert_weight, tower_weight, tower_out, cotangent):
@@ -427,12 +452,12 @@
     tl = nt // m
     step = 512 if units % 512 == 0 else units
     wide = -(-max(rows, ft) // 128) * 128
-    each = 2
+    each = 4
     chunks = m * each
     depth = width // chunks
     hbm = pl.BlockSpec(memory_space=pltpu.HBM)
     dma = pltpu.SemaphoreType.DMA
-    return tuple(pl.pallas_call(
+    pred, grad = pl.pallas_call(
         functools.partial(kernel, n, nt, m),
         out_shape=(
             jax.ShapeDtypeStruct((1, nt * rows), F32),
@@ -451,6 +476,7 @@
             pltpu.VMEM((n, chunks, slots, depth), BF16),
             pltpu.VMEM((n, chunks, slots, depth), BF16),
             pltpu.VMEM((n, rows, slots), BF16),
+            pltpu.VMEM((slots, units), F32),
             pltpu.VMEM((slots, units), F32),
             pltpu.VMEM((slots, units), BF16),
             pltpu.VMEM((n, tl, slots, ft), F32),
@@ -479,7 +505,19 @@
         compiler_params=pltpu.CompilerParams(
             collective_id=0, has_side_effects=True, vmem_limit_bytes=60 * 1024 * 1024),
         name="expert_towers",
-    )(tokens, expert_ids.T, gate_levels.T, expert_weight, tower_weight, tower_out, cotangent))
+    )(tokens, expert_ids.T, gate_levels.T, expert_weight, tower_weight, tower_out, cotangent)
+    return tuple(pl.pallas_call(
+        hand_over,
+        out_shape=(
+            jax.ShapeDtypeStruct(pred.shape, F32),
+            jax.ShapeDtypeStruct(grad.shape, BF16),
+        ),
+        in_specs=[hbm] * 2,
+        out_specs=(hbm, hbm),
+        scratch_shapes=[dma((5,))],
+        compiler_params=pltpu.CompilerParams(vmem_limit_bytes=60 * 1024 * 1024),
+        name="hand_over",
+    )(pred, grad))
 
 
 def solution(mesh):

time: 58.9 us -> 79.4 us (1.35)
  Pallas kernels: 54.8 us -> 78.6 us
  local copies, waits for them, and re-layouts: 3.34 us -> 0 us
    pallas_call x0 -> x1, Pallas kernels: none -> 25.1 us  [body(): pl.pallas_call(hand_over, out_shape=(jax.ShapeDtypeStruct(pred.shape, F32...]
    unnamed x2 -> x0, local copies, waits for them, and re-layouts: 3.34 us -> none
    pallas_call x1, Pallas kernels: 54.8 us -> 53.6 us  [body(): pl.pallas_call(functools.partial(kernel, n, nt, m), out_shape=(jax.ShapeD...]
where the time goes in v4:
time: 79.4 us; the launch traced here: 79.3 us
  Pallas kernels  78.6 us (99%)
    pallas_call x1, Pallas kernels, body(): pl.pallas_call(functools.partial(kernel, n, nt, m), out_shape=(jax.ShapeD...  53.6 us
    pallas_call x1, Pallas kernels, body(): pl.pallas_call(hand_over, out_shape=(jax.ShapeDtypeStruct(pred.shape, F32...  25.1 us

profile of v4, /device:TPU:0, one launch (start us, length us, event | category | flops | bytes accessed | tf_op | source)
XLA Modules:
  0.0 79.3 jit_solution(3821512643516519471)
XLA Ops:
  0.6 53.6 %expert_towers.1 = (f32[1,768]{1,0:T(1,128)}, bf16[192,2048]{1,0:T(8,128)(2,1)}) custom-call(bf16[192,2048]{1,0:T(8,128)(2,1)} %tokens.1, s32[2,192]{1,0:T(2,128)} %bitcast.2, s32[2,192]{1,0:T(2,128)} %bitcast.3, bf16[1,2048,2048]{2,1,0:T(8,128)(2,1)} %weight.1, bf16[4,2048,256]{2,1,0:T(8,128)(2,1)} %towers.1, f32[1,256]{1,0:T(1,128)} %tower_out_in.1, ...), custom_call_target="tpu_custom_call" | custom-call | tf_op jit(solution)/shard_map/expert_towers/pallas_call | solution.py:460
  54.2 25.1 %hand_over.1 = (f32[1,768]{1,0:T(1,128)}, bf16[192,2048]{1,0:T(8,128)(2,1)}) custom-call(f32[1,768]{1,0:T(1,128)} %get-tuple-element.4.pred, bf16[192,2048]{1,0:T(8,128)(2,1)} %get-tuple-element.5.grad), custom_call_target="tpu_custom_call" | custom-call | tf_op jit(solution)/shard_map/hand_over/pallas_call | solution.py:509

commit v5 on v4

--- a/solution.py
+++ b/solution.py
@@ -118,11 +118,12 @@
 
     fill(2, xi * each, each)
     pl.semaphore_wait(barrier, n - 1 + nt * m - 1)
+    dispatch_copy(2, xi * each).start()
+    fill(1, 0, chunks)
     for q in range(each):
-        dispatch_copy(2, xi * each + q).start()
-    fill(1, 0, chunks)
-    for c in range(chunks):
-        dispatch_copy(1, c).start()
+        if q > 0:
+            dispatch_copy(2, xi * each + q).start()
+        dispatch_copy(1, q).start()
 
     def fill_rest(o, c):
         fill(o, xi * each, each)
@@ -236,15 +237,30 @@
             back_copy(s, l).start()
 
     accumulate(pre, zi, range(chunks), fresh=True, finish=True)
+    for q in range(each):
+        dispatch_copy(3, own_chunk(q)).start()
+        for c in range(each + q * (m - 1), each + (q + 1) * (m - 1)):
+            dispatch_copy(1, c).start()
+    forward(2, 0)
     tower_sums(zi)
+    forward(2, 1)
 
     def work(o, c):
         s = partner(o)
-        for q in range(each):
-            dispatch_copy(o, own_chunk(q)).wait_send()
-            dispatch_copy(o + 1, own_chunk(q)).start()
-        for q in range(each):
-            forward(o, q)
+
+        @pl.when(o + 2 < n)
+        def _():
+            for q in range(each):
+                dispatch_copy(o, own_chunk(q)).wait_send()
+                dispatch_copy(o + 2, own_chunk(q)).start()
+
+        @pl.when(o > 2)
+        def _():
+            forward(o, 0)
+            forward(o, 1)
+
+        forward(o, 2)
+        forward(o, 3)
 
         @pl.when(o > 2)
         def _():
@@ -407,6 +423,7 @@
     for c in range(chunks):
         dispatch_copy(1, c).wait_send()
     for q in range(each):
+        dispatch_copy(n - 2, xi * each + q).wait_send()
         dispatch_copy(n - 1, xi * each + q).wait_send()
     for p in range(1, m):
         for l in range(tl):
@@ -430,16 +447,21 @@
     pred_write.wait()
 
 
-def hand_over(pred, grad, pred_out, grad_out, sem):
+def hand_over(pred, grad, pred_out, grad_out, pred_here, grad_here, sem):
     rows = grad.shape[0] // 4
-    copies = [pltpu.make_async_copy(pred, pred_out, sem.at[4])]
+    parts = [(pred, pred_here, pred_out)]
     for i in range(4):
         at = pl.ds(i * rows, rows)
-        copies.append(pltpu.make_async_copy(grad.at[at, :], grad_out.at[at, :], sem.at[i]))
-    for copy in copies:
-        copy.start()
-    for copy in copies:
-        copy.wait()
+        parts.append((grad.at[at, :], grad_here.at[at, :], grad_out.at[at, :]))
+    reads = [pltpu.make_async_copy(a, b, sem.at[0, i]) for i, (a, b, _) in enumerate(parts)]
+    writes = [pltpu.make_async_copy(b, c, sem.at[1, i]) for i, (_, b, c) in enumerate(parts)]
+    for read in reads:
+        read.start()
+    for read, write in zip(reads, writes):
+        read.wait()
+        write.start()
+    for write in writes:
+        write.wait()
 
 
 def body(tokens, expert_ids, gate_levels, expert_weight, tower_weight, tower_out, cotangent):
@@ -514,7 +536,8 @@
         ),
         in_specs=[hbm] * 2,
         out_specs=(hbm, hbm),
-        scratch_shapes=[dma((5,))],
+        scratch_shapes=[
+            pltpu.VMEM(pred.shape, F32), pltpu.VMEM(grad.shape, BF16), dma((2, 5))],
         compiler_params=pltpu.CompilerParams(vmem_limit_bytes=60 * 1024 * 1024),
         name="hand_over",
     )(pred, grad))

time: 79.4 us -> 56.4 us (0.71); the launches traced: 79.3 us -> 55.4 us
  Pallas kernels: 78.6 us -> 54.8 us
    pallas_call x1, Pallas kernels: 25.1 us -> 1.99 us  [body(): pl.pallas_call(hand_over, out_shape=(jax.ShapeDtypeStruct(pred.shape, F32...]
where the time goes in v5:
time: 56.4 us; the launch traced here: 55.4 us
  Pallas kernels  54.8 us (97%)
  between operations  0.64 us (1%)
    pallas_call x1, Pallas kernels, body(): pl.pallas_call(functools.partial(kernel, n, nt, m), out_shape=(jax.ShapeD...  52.8 us
    pallas_call x1, Pallas kernels, body(): pl.pallas_call(hand_over, out_shape=(jax.ShapeDtypeStruct(pred.shape, F32...  1.99 us

profile of v5, /device:TPU:0, one launch (start us, length us, event | category | flops | bytes accessed | tf_op | source)
XLA Modules:
  0.0 55.4 jit_solution(15517772637955256434)
XLA Ops:
  0.6 52.8 %expert_towers.1 = (f32[1,768]{1,0:T(1,128)}, bf16[192,2048]{1,0:T(8,128)(2,1)}) custom-call(bf16[192,2048]{1,0:T(8,128)(2,1)} %tokens.1, s32[2,192]{1,0:T(2,128)} %bitcast.2, s32[2,192]{1,0:T(2,128)} %bitcast.3, bf16[1,2048,2048]{2,1,0:T(8,128)(2,1)} %weight.1, bf16[4,2048,256]{2,1,0:T(8,128)(2,1)} %towers.1, f32[1,256]{1,0:T(1,128)} %tower_out_in.1, ...), custom_call_target="tpu_custom_call" | custom-call | tf_op jit(solution)/shard_map/expert_towers/pallas_call | solution.py:482
  53.4 2.0 %hand_over.1 = (f32[1,768]{1,0:T(1,128)}, bf16[192,2048]{1,0:T(8,128)(2,1)}) custom-call(f32[1,768]{1,0:T(1,128)} %get-tuple-element.4.pred, bf16[192,2048]{1,0:T(8,128)(2,1)} %get-tuple-element.5.grad), custom_call_target="tpu_custom_call" | custom-call | tf_op jit(solution)/shard_map/hand_over/pallas_call | solution.py:531

commit v6 on v5

--- a/solution.py
+++ b/solution.py
@@ -130,12 +130,10 @@
         return c
 
     lax.fori_loop(3, n, fill_rest, 0)
-
-    for copy in small_loads:
-        copy.wait()
-    for k in range(nt):
-        small_out[k, 0:1, 0:rows] = cotangent[0:1, k * rows:(k + 1) * rows]
-        small_out[k, 1:2, 0:ft] = tower_out[0:1, :]
+    for q in range(each):
+        dispatch_copy(3, xi * each + q).start()
+        for c in range(each + q * (m - 1), each + (q + 1) * (m - 1)):
+            dispatch_copy(1, c).start()
 
     def small_copy(o, arriving=False):
         k = (ti + o) % nt
@@ -144,25 +142,14 @@
             send_sem=s_send.at[k], recv_sem=s_recv.at[k if arriving else ti],
             device_id={"task": k}, device_id_type=MESH)
 
-    def send_small(o, c):
-        small_copy(o).start()
-        return c
-
-    lax.fori_loop(1, nt, send_small, 0)
-    small_in[ti] = small_out[ti]
-
     own = pick(zi)
     for c in range(chunks):
         held[zi, c] = gathered(own, c)
 
-    def set_gate(d, c):
+    def set_gate(d):
         hit = slot_across == column(row_of(place, d))
         gate[d] = jnp.where(hit, column(row_of(level_of, d)), 0.0).astype(BF16)
-        return c
-
-    lax.fori_loop(0, n, set_gate, 0)
-    scale = 1.0 / column(jnp.sum(level_of, axis=0, keepdims=True))
-    zsum[...] = jnp.zeros_like(zsum)
+
     w_load.wait()
     tw_load.wait()
 
@@ -237,14 +224,23 @@
             back_copy(s, l).start()
 
     accumulate(pre, zi, range(chunks), fresh=True, finish=True)
-    for q in range(each):
-        dispatch_copy(3, own_chunk(q)).start()
-        for c in range(each + q * (m - 1), each + (q + 1) * (m - 1)):
-            dispatch_copy(1, c).start()
     forward(2, 0)
     tower_sums(zi)
     forward(2, 1)
 
+    for copy in small_loads:
+        copy.wait()
+    for k in range(nt):
+        small_out[k, 0:1, 0:rows] = cotangent[0:1, k * rows:(k + 1) * rows]
+        small_out[k, 1:2, 0:ft] = tower_out[0:1, :]
+
+    def send_small(o, c):
+        small_copy(o).start()
+        return c
+
+    lax.fori_loop(1, nt, send_small, 0)
+    small_in[ti] = small_out[ti]
+
     def work(o, c):
         s = partner(o)
 
@@ -267,6 +263,7 @@
             send_back(partner(o - 1))
 
         accumulate(pre, s, [own_chunk(q) for q in range(each)], fresh=True)
+        set_gate(s)
         for q in range(each):
             wait_others(s, q)
         accumulate(
@@ -288,6 +285,7 @@
     forward(n - 1, 0)
     forward(n - 1, 1)
     send_back(partner(n - 2))
+    set_gate(last)
     near_group(0)
     forward(n - 1, 2)
     wait_others(last, 0)
@@ -296,11 +294,15 @@
     forward(n - 1, 3)
     near_group(2)
     tower_sums(near)
+    set_gate(near)
     wait_others(last, 1)
     wait_others(last, 2)
     accumulate(
         pre, last, [own_chunk(2), own_chunk(3)] + other_chunks(1) + other_chunks(2))
     send_back(near)
+    set_gate(zi)
+    scale = 1.0 / column(jnp.sum(level_of, axis=0, keepdims=True))
+    zsum[...] = jnp.zeros_like(zsum)
     wait_others(last, 3)
     accumulate(pre, last, other_chunks(3), finish=True)
     tower_sums(last)

time: 56.4 us -> 56.4 us (level)
  no operation moved by 1% of the time
where the time goes in v6:
time: 56.4 us; the launch traced here: 55.6 us
  Pallas kernels  54.9 us (97%)
  between operations  0.64 us (1%)
    pallas_call x1, Pallas kernels, body(): pl.pallas_call(functools.partial(kernel, n, nt, m), out_shape=(jax.ShapeD...  53 us
    pallas_call x1, Pallas kernels, body(): pl.pallas_call(hand_over, out_shape=(jax.ShapeDtypeStruct(pred.shape, F32...  1.99 us

profile of v6, /device:TPU:0, one launch (start us, length us, event | category | flops | bytes accessed | tf_op | source)
XLA Modules:
  0.0 55.6 jit_solution(17132701642334343871)
XLA Ops:
  0.6 53.0 %expert_towers.1 = (f32[1,768]{1,0:T(1,128)}, bf16[192,2048]{1,0:T(8,128)(2,1)}) custom-call(bf16[192,2048]{1,0:T(8,128)(2,1)} %tokens.1, s32[2,192]{1,0:T(2,128)} %bitcast.2, s32[2,192]{1,0:T(2,128)} %bitcast.3, bf16[1,2048,2048]{2,1,0:T(8,128)(2,1)} %weight.1, bf16[4,2048,256]{2,1,0:T(8,128)(2,1)} %towers.1, f32[1,256]{1,0:T(1,128)} %tower_out_in.1, ...), custom_call_target="tpu_custom_call" | custom-call | tf_op jit(solution)/shard_map/expert_towers/pallas_call | solution.py:484
  53.6 2.0 %hand_over.1 = (f32[1,768]{1,0:T(1,128)}, bf16[192,2048]{1,0:T(8,128)(2,1)}) custom-call(f32[1,768]{1,0:T(1,128)} %get-tuple-element.4.pred, bf16[192,2048]{1,0:T(8,128)(2,1)} %get-tuple-element.5.grad), custom_call_target="tpu_custom_call" | custom-call | tf_op jit(solution)/shard_map/hand_over/pallas_call | solution.py:533

commit v7 on v6

--- a/solution.py
+++ b/solution.py
@@ -52,8 +52,6 @@
     tok_loads = [
         load(tokens.at[:, pl.ds(c * depth, depth)], tok.at[c], 6 + c) for c in range(chunks)]
     small_loads = [load(tower_out_in, tower_out, 2), load(cotangent_in, cotangent, 3)]
-    w_load = load(weight.at[0], w, 4)
-    tw_load = load(towers, tw, 5)
 
     barrier = pltpu.get_barrier_semaphore()
 
@@ -102,6 +100,8 @@
 
     for copy in tok_loads:
         copy.wait()
+    w_load = load(weight.at[0], w, 4)
+    tw_load = load(towers, tw, 5)
 
     def dispatch_copy(o, c, arriving=False):
         d = partner(o)

time: 56.4 us -> 56.4 us (level)
  no operation moved by 1% of the time
where the time goes in v7:
time: 56.4 us; the launch traced here: 55.6 us
  Pallas kernels  54.9 us (97%)
  between operations  0.64 us (1%)
    pallas_call x1, Pallas kernels, body(): pl.pallas_call(functools.partial(kernel, n, nt, m), out_shape=(jax.ShapeD...  53 us
    pallas_call x1, Pallas kernels, body(): pl.pallas_call(hand_over, out_shape=(jax.ShapeDtypeStruct(pred.shape, F32...  1.99 us

profile of v7, /device:TPU:0, one launch (start us, length us, event | category | flops | bytes accessed | tf_op | source)
XLA Modules:
  0.0 55.6 jit_solution(11060126757757356963)
XLA Ops:
  0.6 53.0 %expert_towers.1 = (f32[1,768]{1,0:T(1,128)}, bf16[192,2048]{1,0:T(8,128)(2,1)}) custom-call(bf16[192,2048]{1,0:T(8,128)(2,1)} %tokens.1, s32[2,192]{1,0:T(2,128)} %bitcast.2, s32[2,192]{1,0:T(2,128)} %bitcast.3, bf16[1,2048,2048]{2,1,0:T(8,128)(2,1)} %weight.1, bf16[4,2048,256]{2,1,0:T(8,128)(2,1)} %towers.1, f32[1,256]{1,0:T(1,128)} %tower_out_in.1, ...), custom_call_target="tpu_custom_call" | custom-call | tf_op jit(solution)/shard_map/expert_towers/pallas_call | solution.py:484
  53.6 2.0 %hand_over.1 = (f32[1,768]{1,0:T(1,128)}, bf16[192,2048]{1,0:T(8,128)(2,1)}) custom-call(f32[1,768]{1,0:T(1,128)} %get-tuple-element.4.pred, bf16[192,2048]{1,0:T(8,128)(2,1)} %get-tuple-element.5.grad), custom_call_target="tpu_custom_call" | custom-call | tf_op jit(solution)/shard_map/hand_over/pallas_call | solution.py:533
